TPU v7x, 32 devices: a whole 2x2x4 slice. The times are simulated.
32 devices in a mesh: groups: 2 (over x), grid: 16 (over z, y, core).
Axes of the slice: x: 2, y: 2, z: 4, core: 2. Of those that a mesh axis runs over, the one named last changes fastest.
Arguments:
- ensemble: bfloat16 [1024, 128, 128], P(('groups', 'grid')), parts along dimension 0, may hold values from -8 to 8, as said below
- owner_slot: int32 [256], P('groups'), parts along dimension 0, may hold values from 0 to 127, each once
- weights: float32 [256, 64, 64], P(('groups', 'grid')), parts along dimension 0, may hold values from -0.25 to 1.25, as said below
- obs_members: bfloat16 [1024, 64, 128], P(('groups', 'grid')), parts along dimension 0, may hold values from -2 to 2
- departures: bfloat16 [1024, 128], P(('groups', 'grid')), parts along dimension 0, may hold values from -6 to 6
- obs_count: int32 [1024], P(('groups', 'grid')), parts along dimension 0, may hold values from 1 to 128, 40960 in all
- pair_home: int32 [256, 8], P('groups'), parts along dimension 0, may hold values from 0 to 15, all different within a row; in each aligned block of 8 rows (0 to 7, 8 to 15, ...) at most 8 rows name the same one
- pair_index: int32 [256, 8], P('groups'), parts along dimension 0, may hold values from 0 to 31
- localization: float32 [256, 8], P(('groups', 'grid')), parts along dimension 0, may hold values from 0.2 to 1
Outputs:
- analysis: bfloat16 [1024, 128, 128], P(('groups', 'grid')), parts along dimension 0
- mean_weights: float32 [256, 64], P(('groups', 'grid')), parts along dimension 0
There are 2 independent parts, one for each index of `groups`. A program takes and returns all parts, laid end to end along the dimension named above; each array names one. Nothing has to cross between parts.
Inputs may be any that keep to these rules, and one draw needn't show every extreme that they name: The ensemble is a common field plus member perturbations. `weights`: dominant diagonal with full off-diagonal part. `pair_home`: each slot's 8 pairs name different home devices; among the 8 slots of one device no home device is named by more than 8 pairs. `owner_slot`: each slot once.
All inputs are finite; a program needn't handle non-finite values. No bound on the sum of `obs_count` on one device may be relied on, other than what follows from the above.
Results may differ from a plain program's by a relative error of at most 0.0075.
Values may be sent and summed in bfloat16 or wider, within the bound.
A program may use at most 64 MiB of HBM per device.

v0:
```python
import jax
import jax.numpy as jnp
from jax import lax
from jax.sharding import PartitionSpec as P

LEV = 8


def per_device(
    ensemble,
    owner_slot,
    weights,
    obs_members,
    departures,
    obs_count,
    pair_home,
    pair_index,
    localization,
):
    devices = lax.axis_size("grid")
    my_index = lax.axis_index("grid")
    rows_here, blocks_all, points = ensemble.shape
    block_dev = weights.shape[0]
    members = weights.shape[1]
    pair_count = pair_home.shape[1]
    entries = block_dev * pair_count
    capacity = max(2, 2 * entries // devices)
    slot_pos = lax.broadcasted_iota(jnp.int32, departures.shape, 1)
    masked = jnp.where(slot_pos < obs_count[:, None], departures, jnp.zeros_like(departures))
    homes_all = pair_home.reshape(devices, entries)
    index_all = pair_index.reshape(devices, entries)
    matches = homes_all == my_index
    position = jnp.cumsum(matches.astype(jnp.int32), axis=1) - 1
    slot_ids = jnp.arange(capacity, dtype=jnp.int32)
    select = matches[:, None, :] & (position[:, None, :] == slot_ids[None, :, None])
    picked = jnp.sum(jnp.where(select, index_all[:, None, :], 0), axis=2)
    filled = jnp.any(select, axis=2)
    own_sums = jnp.einsum("okp,op->ok", obs_members, masked, preferred_element_type=jnp.float32)
    send_sums = jnp.where(filled[:, :, None], own_sums[picked], jnp.zeros((), jnp.float32))
    received = lax.all_to_all(send_sums, "grid", split_axis=0, concat_axis=0, tiled=True).reshape(
        devices * capacity, members
    )
    first_row = my_index * block_dev
    my_homes = lax.dynamic_slice_in_dim(pair_home, first_row, block_dev, 0).reshape(entries)
    order_row = lax.broadcasted_iota(jnp.int32, (entries, entries), 0)
    order_col = lax.broadcasted_iota(jnp.int32, (entries, entries), 1)
    earlier = (my_homes[:, None] == my_homes[None, :]) & (order_col < order_row)
    my_position = jnp.sum(earlier.astype(jnp.int32), axis=1)
    item_index = my_homes * capacity + my_position
    pair_sums = received[item_index].reshape(block_dev, pair_count, members)
    innovation = jnp.sum(localization[:, :, None] * pair_sums, axis=1)
    projected = jnp.einsum("bmi,bm->bi", weights, innovation, precision=lax.Precision.HIGHEST)
    mean_weights = jnp.einsum("bji,bi->bj", weights, projected, precision=lax.Precision.HIGHEST) / (
        members - 1
    )
    transform = (weights + mean_weights[:, :, None]).astype(jnp.bfloat16)
    column_totals = jnp.sum(transform.astype(jnp.float32), axis=1)
    inverse = (
        jnp.zeros((blocks_all,), jnp.int32)
        .at[owner_slot]
        .set(jnp.arange(blocks_all, dtype=jnp.int32))
    )
    ordered = ensemble[:, inverse, :]
    owned = lax.all_to_all(ordered, "grid", split_axis=1, concat_axis=0, tiled=True)
    states = owned.reshape(members, LEV, block_dev, points)
    ens_mean = jnp.sum(states, axis=0, dtype=jnp.float32) / members
    product = jnp.einsum("jlbp,bji->ilbp", states, transform, preferred_element_type=jnp.float32)
    analysis = (product + ens_mean[None] * (1.0 - column_totals).T[:, None, :, None]).astype(
        jnp.bfloat16
    )
    returned = lax.all_to_all(
        analysis.reshape(members * LEV, block_dev, points),
        "grid",
        split_axis=0,
        concat_axis=1,
        tiled=True,
    )
    result = returned[:, owner_slot, :]
    return (result, mean_weights)


def solution(mesh):
    placed = (
        P(("groups", "grid"), None, None),
        P("groups"),
        P(("groups", "grid"), None, None),
        P(("groups", "grid"), None, None),
        P(("groups", "grid"), None),
        P(("groups", "grid")),
        P("groups", None),
        P("groups", None),
        P(("groups", "grid"), None),
    )
    return jax.shard_map(
        per_device,
        mesh=mesh,
        in_specs=placed,
        out_specs=(P(("groups", "grid"), None, None), P(("groups", "grid"), None)),
        check_vma=False,
    )
```

profile of v0, /device:TPU:15, one launch (start us, length us, event | category | flops | bytes accessed | tf_op | source)
XLA Modules:
  0.0 89.8 jit_solution(13606325764080355471)
XLA Ops:
  0.6 0.0 copy-start
  0.7 0.8 broadcast_compare_fusion
  1.4 0.1 copy.55
  1.6 0.1 eq.47
  1.7 0.2 reduce_window_sum.11
  1.9 0.8 copy.56
  2.7 0.1 broadcast_in_dim.49
  2.8 0.4 fusion.4
  3.1 0.4 select_reduce_fusion
  3.5 0.1 copy.57
  3.6 0.1 copy.58
  3.6 0.1 reshape.96
  3.8 0.8 fusion.10
  4.5 1.4 %fusion.7 = f32[32,1,64]{2,1,0:T(1,128)S(1)} fusion(bf16[32,64,128]{2,1,0:T(8,128)(2,1)} %param.12, bf16[32,128,1]{1,0,2:T(8,128)(2,1)S(1)} %fusion.10), kind=kOutput, calls=%fused_computation.24 | convolution fusion | flops 524288 | bytes 540672 | tf_op jit(solution)/shard_map/okp,op->ok/dot_general | solution.py:38
  5.9 0.7 gather_fusion
  6.6 0.1 bitcast_select_fusion
  6.7 0.7 reshape.147
  7.4 6.6 %all-to-all-start = ((f32[16,1,512]{2,1,0:T(1,128)}), f32[16,1,512]{2,1,0:T(1,128)S(1)}, u32[]{:S(2)}, u32[]{:S(2)}) async-start(f32[16,1,512]{2,1,0:T(1,128)} %reshape.147), calls=%async_computation | async-start | bytes 65536 | tf_op jit(solution)/shard_map/all_to_all | solution.py:40
  14.0 1.0 %scatter_custom_fusion = s32[128]{0:T(128)S(1)} fusion(s32[128]{0:T(128)S(1)} %compare_select_fusion.2, s32[128]{0:T(128)S(1)} %iota.25, s32[]{:T(128)} %constant.13.clone.1), kind=kCustom, calls=%fused_computation.45 | custom fusion | bytes 516 | tf_op jit(solution)/shard_map/scatter | solution.py:61
  15.0 5.2 %gather_fusion.2 = bf16[128,32,128]{2,0,1:T(8,128)(2,1)S(1)} fusion(bf16[32,128,128]{2,1,0:T(8,128)(2,1)S(1)} %copy-done, s32[1024]{0:T(1024)S(1)} %pad_clamp_fusion.1), kind=kCustom, calls=%fused_computation.2 | custom fusion | bytes 2097664 | tf_op jit(solution)/shard_map/gather | solution.py:63
  20.2 1.6 %copy.61 = bf16[32,128,128]{2,0,1:T(8,128)(2,1)} copy(bf16[32,128,128]{2,1,0:T(8,128)(2,1)S(1)} %bitcast.64) | data formatting | bytes 2097152 | tf_op jit(solution)/shard_map/gather | solution.py:63
  21.8 0.0 all-to-all-done
  21.8 6.2 %all-to-all-start.1 = ((bf16[32,128,128]{2,0,1:T(8,128)(2,1)}), bf16[32,128,128]{2,0,1:T(8,128)(2,1)S(1)}, u32[]{:S(2)}, u32[]{:S(2)}) async-start(bf16[32,128,128]{2,0,1:T(8,128)(2,1)} %copy.61), calls=%async_computation.1 | async-start | bytes 2097152 | tf_op jit(solution)/shard_map/all_to_all | solution.py:64
  28.0 0.1 broadcast_multiply_fusion.2
  28.1 0.1 copy.60
  28.2 0.1 eq.51
  28.2 0.1 copy.59
  28.3 0.1 mul.44
  28.4 0.2 convert_reduce_fusion.2
  28.6 0.5 broadcast.100
  29.1 0.7 reduce
  29.8 0.1 reshape.148
  29.9 0.6 gather_fusion.1
  30.5 0.1 fusion.5
  30.6 0.3 convolution_bitcast_fusion
  30.9 0.5 fusion.14
  31.5 0.2 convert_reduce_fusion.1
  31.6 21.2 %all-to-all-done.1 = bf16[32,128,128]{2,0,1:T(8,128)(2,1)S(1)} async-done(((bf16[32,128,128]{2,0,1:T(8,128)(2,1)}), bf16[32,128,128]{2,0,1:T(8,128)(2,1)S(1)}, u32[]{:S(2)}, u32[]{:S(2)}) %all-to-all-start.1) | async-done | bytes 1048608 | tf_op jit(solution)/shard_map/all_to_all | solution.py:64
  52.9 0.5 copy.63
  53.3 0.2 convert_reduce_fusion
  53.6 1.6 %fusion = bf16[64,8,8,128]{3,0,1,2:T(8,128)(2,1)S(1)} fusion(bf16[64,8,8,128]{3,2,1,0:T(8,128)(2,1)S(1)} %bitcast.63, f32[64,8]{0,1:T(8,128)S(1)} %subtract_bitcast_fusion, f32[8,8,128]{2,0,1:T(8,128)S(1)} %copy.66, f32[8,64,64]{2,1,0:T(8,128)S(1)} %copy-done.1, f32[8,64]{1,0:T(8,128)S(1)} %broadcast_multiply_fusion.1), kind=kOutput, calls=%fused_computation.6 | convolution fusion | flops 68747264 | bytes 2265088 | tf_op jit(solution)/shard_map/jlbp,bji->ilbp/dot_general | solution.py:67
  55.2 1.6 %copy.67 = bf16[64,8,8,128]{3,2,1,0:T(8,128)(2,1)} copy(bf16[64,8,8,128]{3,0,1,2:T(8,128)(2,1)S(1)} %fusion) | data formatting | bytes 2097152 | tf_op jit(solution)/shard_map/convert_element_type | solution.py:68
  56.9 4.9 %all-to-all-start.2 = ((bf16[512,8,128]{2,1,0:T(8,128)(2,1)}), bf16[512,8,128]{2,1,0:T(8,128)(2,1)S(1)}, u32[]{:S(2)}, u32[]{:S(2)}) async-start(bf16[512,8,128]{2,1,0:T(8,128)(2,1)} %bitcast.25), calls=%async_computation.2 | async-start | bytes 2097152 | tf_op jit(solution)/shard_map/all_to_all | solution.py:71
  61.8 24.9 %all-to-all-done.2 = bf16[512,8,128]{2,1,0:T(8,128)(2,1)S(1)} async-done(((bf16[512,8,128]{2,1,0:T(8,128)(2,1)}), bf16[512,8,128]{2,1,0:T(8,128)(2,1)S(1)}, u32[]{:S(2)}, u32[]{:S(2)}) %all-to-all-start.2) | async-done | bytes 1048608 | tf_op jit(solution)/shard_map/all_to_all | solution.py:71
  86.7 0.3 copy.86
  87.0 0.7 copy.69
  87.6 0.8 gather_fusion.3
  88.4 1.4 %copy.70 = bf16[32,128,128]{2,1,0:T(8,128)(2,1)} copy(bf16[32,128,128]{2,0,1:T(8,128)(2,1)S(1)} %bitcast.65) | data formatting | bytes 2097152
  (26 shorter events, 0.1 us)
Async XLA Ops:
  0.6 14.4 %copy-start = (bf16[32,128,128]{2,1,0:T(8,128)(2,1)S(1)}, bf16[32,128,128]{2,1,0:T(8,128)(2,1)}, u32[]{:S(2)}) copy-start(bf16[32,128,128]{2,1,0:T(8,128)(2,1)} %param.9) | copy-start | bytes 3145732
  0.6 13.3 %copy-start.5 = (s32[128]{0:T(128)S(1)}, s32[128]{0:T(128)}, u32[]{:S(2)}) copy-start(s32[128]{0:T(128)} %param.10) | copy-start | bytes 1540
  7.4 14.5 %all-to-all-start = ((f32[16,1,512]{2,1,0:T(1,128)}), f32[16,1,512]{2,1,0:T(1,128)S(1)}, u32[]{:S(2)}, u32[]{:S(2)}) async-start(f32[16,1,512]{2,1,0:T(1,128)} %reshape.147), calls=%async_computation | async-start | bytes 65536 | tf_op jit(solution)/shard_map/all_to_all | solution.py:40
  21.8 6.2 %copy-start.3 = (s32[128,8]{0,1:T(8,128)S(1)}, s32[128,8]{0,1:T(8,128)}, u32[]{:S(2)}) copy-start(s32[128,8]{0,1:T(8,128)} %param.15) | copy-start | bytes 12292
  21.8 8.7 %copy-start.4 = (f32[8,8]{1,0:T(8,128)S(1)}, f32[8,8]{1,0:T(8,128)}, u32[]{:S(2)}) copy-start(f32[8,8]{1,0:T(8,128)} %param.17) | copy-start | bytes 772
  21.8 8.8 %copy-start.1 = (f32[8,64,64]{2,1,0:T(8,128)S(1)}, f32[8,64,64]{2,1,0:T(8,128)}, u32[]{:S(2)}) copy-start(f32[8,64,64]{2,1,0:T(8,128)} %param.11) | copy-start | bytes 393220
  21.8 31.0 %all-to-all-start.1 = ((bf16[32,128,128]{2,0,1:T(8,128)(2,1)}), bf16[32,128,128]{2,0,1:T(8,128)(2,1)S(1)}, u32[]{:S(2)}, u32[]{:S(2)}) async-start(bf16[32,128,128]{2,0,1:T(8,128)(2,1)} %copy.61), calls=%async_computation.1 | async-start | bytes 2097152 | tf_op jit(solution)/shard_map/all_to_all | solution.py:64
  31.5 22.1 %copy-start.2 = (f32[8,64]{1,0:T(8,128)}, f32[8,64]{1,0:T(8,128)S(1)}, u32[]{:S(2)}) copy-start(f32[8,64]{1,0:T(8,128)S(1)} %broadcast_multiply_fusion.1) | copy-start | bytes 6148
  56.9 29.8 %all-to-all-start.2 = ((bf16[512,8,128]{2,1,0:T(8,128)(2,1)}), bf16[512,8,128]{2,1,0:T(8,128)(2,1)S(1)}, u32[]{:S(2)}, u32[]{:S(2)}) async-start(bf16[512,8,128]{2,1,0:T(8,128)(2,1)} %bitcast.25), calls=%async_computation.2 | async-start | bytes 2097152 | tf_op jit(solution)/shard_map/all_to_all | solution.py:71
where the time goes:
time: 90.3 us; the launch traced here: 89.8 us
  waiting for transfers between devices  46.1 us (51%)
  starting transfers between devices  17.7 us (20%)
  local copies, waits for them, and re-layouts  17.3 us (19%)
  other arithmetic  4.03 us (4%)
  matrix products  3.88 us (4%)
    all_to_all x1, waiting for transfers between devices, per_device(): lax.all_to_all(analysis.reshape(members * LEV, block_dev, points), 'grid'...  24.9 us
    all_to_all x1, waiting for transfers between devices, per_device(): lax.all_to_all(ordered, 'grid', split_axis=1, concat_axis=0, tiled=True)  21.2 us
    gather x2, local copies, waits for them, and re-layouts, per_device(): ordered = ensemble[:, inverse, :]  6.84 us
    all_to_all x1, starting transfers between devices, per_device(): lax.all_to_all(send_sums, 'grid', split_axis=0, concat_axis=0, tiled=True)  6.55 us
    all_to_all x1, starting transfers between devices, per_device(): lax.all_to_all(ordered, 'grid', split_axis=1, concat_axis=0, tiled=True)  6.16 us
    all_to_all x1, starting transfers between devices, per_device(): lax.all_to_all(analysis.reshape(members * LEV, block_dev, points), 'grid'...  4.94 us
    unnamed x16, local copies, waits for them, and re-layouts  2.97 us
  transfers between devices with their start and end apart: 3, of which 2 were waited for; matrix products, arithmetic and copies ran while one was open for 13% of the time, Pallas kernels for 0%

commit v1 on v0

--- a/solution.py
+++ b/solution.py
@@ -1,12 +1,320 @@
+import functools
+
 import jax
 import jax.numpy as jnp
 from jax import lax
+from jax.experimental import pallas as pl
+from jax.experimental.pallas import tpu as pltpu
 from jax.sharding import PartitionSpec as P
 
 LEV = 8
-
-
-def per_device(
+LANES = 128
+F32 = jnp.float32
+BF16 = jnp.bfloat16
+HIGHEST = lax.Precision.HIGHEST
+
+
+def iota(shape, dim):
+    return lax.broadcasted_iota(jnp.int32, shape, dim)
+
+
+def one_hot(cond):
+    return jnp.where(cond, 1.0, 0.0).astype(BF16)
+
+
+def dot(a, b):
+    return jnp.dot(a, b, preferred_element_type=F32)
+
+
+def dot_nt(a, b, precision=None):
+    return lax.dot_general(
+        a, b, (((1,), (1,)), ((), ())), preferred_element_type=F32, precision=precision
+    )
+
+
+def peer_order(n):
+    return sorted(range(1, n), key=lambda k: -min(k, n - k))
+
+
+def fused_kernel(
+    dims,
+    ens_ref,
+    owner_ref,
+    weights_ref,
+    obs_ref,
+    dep_ref,
+    count_ref,
+    home_ref,
+    index_ref,
+    loc_ref,
+    out_ref,
+    mw_ref,
+    obs_box,
+    send_box,
+    recv_box,
+    ret_box,
+    back_box,
+    gather_mat,
+    scatter_mat,
+    mix_mat,
+    gain_ref,
+    obs_send,
+    obs_recv,
+    fwd_send,
+    fwd_recv,
+    bwd_send,
+    bwd_recv,
+):
+    n, groups = dims
+    me = lax.axis_index("grid")
+    rows_here, blocks, points = ens_ref.shape
+    block_dev, members, _ = weights_ref.shape
+    obs_dev = obs_ref.shape[0]
+    pair_count = home_ref.shape[1]
+    held = rows_here // LEV
+    slab = held * block_dev
+    full = n * slab
+    lev_group = LEV // groups
+    width = lev_group * points
+    packed = obs_dev // 2
+    peers = peer_order(n)
+
+    barrier = pltpu.get_barrier_semaphore()
+
+    def greet(k, carry):
+        pl.semaphore_signal(
+            barrier,
+            inc=1,
+            device_id={"grid": lax.rem(me + k, n)},
+            device_id_type=pl.DeviceIdType.MESH,
+        )
+        return carry
+
+    lax.fori_loop(1, n, greet, 0)
+
+    lane = iota((obs_dev, points), 1)
+    dep = dep_ref[...].astype(F32)
+    masked = jnp.where(lane < count_ref[...], dep, 0.0).astype(BF16)
+    cross = dot_nt(masked, obs_ref[...].reshape(obs_dev * members, points))
+    row = iota((obs_dev, LANES), 0)
+    lane_block = iota((obs_dev, LANES), 1) // members
+    per_row = LANES // members
+    sums = jnp.zeros((obs_dev, LANES), F32)
+    for t in range(obs_dev * members // LANES):
+        piece = cross[:, t * LANES : (t + 1) * LANES]
+        sums = sums + jnp.where(row == lane_block + t * per_row, piece, 0.0)
+    fold = one_hot(iota((packed, obs_dev), 0) == iota((packed, obs_dev), 1) // 2)
+    obs_box[pl.ds(me, 1)] = dot(fold, sums.astype(BF16)).astype(BF16)[None]
+
+    r = iota((full, 1), 0)
+    row_key = (r // block_dev % held) * blocks + (r // slab) * block_dev + r % block_dev
+    owner = jnp.concatenate([owner_ref[...]] * held, axis=1)
+    col_key = owner + iota((1, full), 1) // blocks * blocks
+    gather_mat[...] = one_hot(row_key == col_key)
+
+    def arrange(g):
+        cols = []
+        for l in range(g * lev_group, (g + 1) * lev_group):
+            cols.append(
+                jnp.concatenate([ens_ref[m * LEV + l] for m in range(held)], axis=0)
+            )
+        state = jnp.concatenate(cols, axis=1)
+        sorted_state = dot(gather_mat[...], state).astype(BF16)
+        send_box[g] = sorted_state.reshape(n, slab, width)
+        recv_box[g, pl.ds(me, 1)] = send_box[g, pl.ds(me, 1)]
+
+    def obs_copy(k):
+        to = lax.rem(me + k, n)
+        return pltpu.make_async_remote_copy(
+            src_ref=obs_box.at[me],
+            dst_ref=obs_box.at[me],
+            send_sem=obs_send.at[k],
+            recv_sem=obs_recv.at[me],
+            device_id={"grid": to},
+            device_id_type=pl.DeviceIdType.MESH,
+        )
+
+    def box_copy(src, dst, send_sem, recv_sem, g, k):
+        to = lax.rem(me + k, n)
+        return pltpu.make_async_remote_copy(
+            src_ref=src.at[g, to],
+            dst_ref=dst.at[g, me],
+            send_sem=send_sem.at[g, k],
+            recv_sem=recv_sem.at[g, me],
+            device_id={"grid": to},
+            device_id_type=pl.DeviceIdType.MESH,
+        )
+
+    def box_arrival(dst, send_sem, recv_sem, g, k):
+        src = lax.rem(me + k, n)
+        return pltpu.make_async_remote_copy(
+            src_ref=dst.at[g, src],
+            dst_ref=dst.at[g, src],
+            send_sem=send_sem.at[g, k],
+            recv_sem=recv_sem.at[g, src],
+            device_id={"grid": src},
+            device_id_type=pl.DeviceIdType.MESH,
+        )
+
+    arrange(0)
+    pl.semaphore_wait(barrier, n - 1)
+    for k in peers:
+        obs_copy(k).start()
+    for k in peers:
+        box_copy(send_box, recv_box, fwd_send, fwd_recv, 0, k).start()
+    for g in range(1, groups):
+        arrange(g)
+        for k in peers:
+            box_copy(send_box, recv_box, fwd_send, fwd_recv, g, k).start()
+
+    same = one_hot(iota((full, full), 0) == iota((full, full), 1))
+    scatter_mat[...] = dot_nt(same, gather_mat[...]).astype(BF16)
+
+    for k in peers:
+        src = lax.rem(me + k, n)
+        pltpu.make_async_remote_copy(
+            src_ref=obs_box.at[src],
+            dst_ref=obs_box.at[src],
+            send_sem=obs_send.at[k],
+            recv_sem=obs_recv.at[src],
+            device_id={"grid": src},
+            device_id_type=pl.DeviceIdType.MESH,
+        ).wait_recv()
+    all_sums = obs_box[...].reshape(n * packed, LANES).astype(F32)
+    mine = pl.ds(pl.multiple_of(me * block_dev, block_dev), block_dev)
+    home = home_ref[mine, :]
+    index = index_ref[mine, :]
+    spot = home * packed + index // 2
+    odd = index % 2
+    loc = loc_ref[...]
+    col = iota((block_dev, n * packed), 1)
+    pick = [jnp.zeros((block_dev, n * packed), F32) for _ in range(2)]
+    for k in range(pair_count):
+        hit = col == spot[:, k : k + 1]
+        for parity in range(2):
+            gate = jnp.where(odd[:, k : k + 1] == parity, loc[:, k : k + 1], 0.0)
+            pick[parity] = pick[parity] + jnp.where(hit, gate, 0.0)
+    even_part = jnp.dot(pick[0], all_sums, precision=HIGHEST, preferred_element_type=F32)
+    odd_part = jnp.dot(pick[1], all_sums, precision=HIGHEST, preferred_element_type=F32)
+    innovation = even_part[:, :members] + odd_part[:, members:]
+
+    weights = weights_ref[...]
+    flat = weights.reshape(block_dev * members, members)
+    twice = jnp.concatenate([innovation, innovation], axis=1)
+    spread = jnp.concatenate([twice] * (block_dev // 2), axis=1)
+    spread_row = iota((block_dev, block_dev * members), 0)
+    spread_col = iota((block_dev, block_dev * members), 1) // members
+    spread = jnp.where(spread_row == spread_col, spread, 0.0)
+    projected = jnp.dot(spread, flat, precision=HIGHEST, preferred_element_type=F32)
+    mean_w = jnp.sum(weights * projected[:, None, :], axis=2, keepdims=True) / (members - 1)
+    mw_ref[...] = jnp.sum(weights * projected[:, None, :], axis=2) / (members - 1)
+    transform = (weights + mean_w).astype(BF16).reshape(block_dev * members, members)
+
+    rr = iota((full, full), 0)
+    cc = iota((full, full), 1)
+    turn = one_hot((rr // block_dev == cc % members) & (rr % block_dev == cc // members))
+    turned = dot(turn, transform).astype(BF16)
+    repeat = one_hot(iota((full, members), 0) // block_dev == iota((full, members), 1))
+    dense = dot_nt(repeat, turned)
+    mix_mat[...] = jnp.where(rr % block_dev == cc % block_dev, dense, 0.0).astype(BF16)
+    totals = dot(mix_mat[...], jnp.ones((full, width), BF16))
+    gain_ref[...] = (1.0 - totals) * (1.0 / members)
+    sum_mat = one_hot(iota((block_dev, full), 0) == iota((block_dev, full), 1) % block_dev)
+
+    for g in range(groups):
+        for k in peers:
+            box_arrival(recv_box, fwd_send, fwd_recv, g, n - k).wait_recv()
+        state = recv_box[g].reshape(full, width)
+        product = dot(mix_mat[...], state).reshape(members, block_dev, width)
+        member_sum = dot(sum_mat, state)
+        gain = gain_ref[...].reshape(members, block_dev, width)
+        analysis = (product + gain * member_sum[None]).astype(BF16)
+        ret_box[g] = analysis.reshape(n, slab, width)
+        back_box[g, pl.ds(me, 1)] = ret_box[g, pl.ds(me, 1)]
+        for k in peers:
+            box_copy(ret_box, back_box, bwd_send, bwd_recv, g, k).start()
+
+    for g in range(groups):
+        for k in peers:
+            box_arrival(back_box, bwd_send, bwd_recv, g, n - k).wait_recv()
+        final = dot(scatter_mat[...], back_box[g].reshape(full, width)).astype(BF16)
+        for l in range(lev_group):
+            for m in range(held):
+                out_ref[m * LEV + g * lev_group + l] = final[
+                    m * blocks : (m + 1) * blocks, l * points : (l + 1) * points
+                ]
+
+    for k in peers:
+        obs_copy(k).wait_send()
+        for g in range(groups):
+            box_copy(send_box, recv_box, fwd_send, fwd_recv, g, k).wait_send()
+            box_copy(ret_box, back_box, bwd_send, bwd_recv, g, k).wait_send()
+
+
+def fused(
+    ensemble,
+    owner_slot,
+    weights,
+    obs_members,
+    departures,
+    obs_count,
+    pair_home,
+    pair_index,
+    localization,
+    groups=4,
+):
+    n = lax.axis_size("grid")
+    rows_here, blocks, points = ensemble.shape
+    block_dev, members, _ = weights.shape
+    held = rows_here // LEV
+    slab = held * block_dev
+    full = n * slab
+    width = LEV // groups * points
+    obs_dev = obs_members.shape[0]
+    box = pltpu.VMEM((groups, n, slab, width), BF16)
+    vmem = pl.BlockSpec(memory_space=pltpu.VMEM)
+    return pl.pallas_call(
+        functools.partial(fused_kernel, (n, groups)),
+        out_shape=(
+            jax.ShapeDtypeStruct(ensemble.shape, BF16),
+            jax.ShapeDtypeStruct((block_dev, members), F32),
+        ),
+        in_specs=[vmem] * 9,
+        out_specs=(vmem, vmem),
+        scratch_shapes=[
+            pltpu.VMEM((n, obs_dev // 2, LANES), BF16),
+            box,
+            box,
+            box,
+            box,
+            pltpu.VMEM((full, full), BF16),
+            pltpu.VMEM((full, full), BF16),
+            pltpu.VMEM((full, full), BF16),
+            pltpu.VMEM((full, width), F32),
+            pltpu.SemaphoreType.DMA((n,)),
+            pltpu.SemaphoreType.DMA((n,)),
+            pltpu.SemaphoreType.DMA((groups, n)),
+            pltpu.SemaphoreType.DMA((groups, n)),
+            pltpu.SemaphoreType.DMA((groups, n)),
+            pltpu.SemaphoreType.DMA((groups, n)),
+        ],
+        compiler_params=pltpu.CompilerParams(
+            collective_id=0, has_side_effects=True, vmem_limit_bytes=40 * 2**20
+        ),
+    )(
+        ensemble,
+        owner_slot.reshape(1, blocks),
+        weights,
+        obs_members,
+        departures,
+        obs_count.reshape(obs_dev, 1),
+        pair_home,
+        pair_index,
+        localization,
+    )
+
+
+def staged(
     ensemble,
     owner_slot,
     weights,
@@ -79,6 +387,15 @@
     return (result, mean_weights)
 
 
+def per_device(ensemble, owner_slot, weights, *rest):
+    rows_here = ensemble.shape[0]
+    block_dev = weights.shape[0]
+    whole_members = rows_here % LEV == 0
+    if whole_members and (rows_here // LEV) * block_dev % 16 == 0:
+        return fused(ensemble, owner_slot, weights, *rest)
+    return staged(ensemble, owner_slot, weights, *rest)
+
+
 def solution(mesh):
     placed = (
         P(("groups", "grid"), None, None),

time: 90.3 us -> 64.7 us (0.72)
  the two profiles are of different devices: /device:TPU:15 before, /device:TPU:0 now
where the time goes in v1:
time: 64.7 us; the launch traced here: 64.4 us
  Pallas kernels  56.2 us (87%)
  local copies, waits for them, and re-layouts  7.5 us (12%)
  between operations  0.66 us (1%)
    pallas_call x1, Pallas kernels, fused(): pl.pallas_call(functools.partial(fused_kernel, (n, groups)), out_shape=(j...  56.2 us
    unnamed x22, local copies, waits for them, and re-layouts  7.42 us

profile of v1, /device:TPU:0, one launch (start us, length us, event | category | flops | bytes accessed | tf_op | source)
XLA Modules:
  0.0 64.4 jit_solution(3344394338046018150)
XLA Ops:
  0.6 0.0 copy-start.8
  0.6 0.6 %copy-done.8 = s32[32]{0:T(128)S(1)} copy-done((s32[32]{0:T(128)S(1)}, s32[32]{0:T(128)}, u32[]{:S(2)}) %copy-start.8) | copy-done | bytes 152
  1.3 0.0 copy-start.6
  1.3 0.1 copy.11.count_ref
  1.4 0.6 copy-done.6
  2.0 0.0 copy-start.7
  2.0 0.1 copy.12.home_ref
  2.1 0.6 copy-done.7
  2.7 0.0 copy-start.3
  2.7 0.0 copy-start.4
  2.7 0.0 copy-start.5
  2.7 0.1 copy.13.index_ref
  2.8 0.6 copy-done.3
  3.4 0.0 copy-done.4
  3.4 0.0 copy-done.5
  3.4 0.0 copy-start
  3.4 1.2 %copy-done = bf16[32,128,128]{2,1,0:T(8,128)(2,1)S(1)} copy-done((bf16[32,128,128]{2,1,0:T(8,128)(2,1)S(1)}, bf16[32,128,128]{2,1,0:T(8,128)(2,1)}, u32[]{:S(2)}) %copy-start) | copy-done | bytes 1048600
  4.6 0.0 copy-start.1
  4.6 1.0 %copy-done.1 = bf16[32,64,128]{2,1,0:T(8,128)(2,1)S(1)} copy-done((bf16[32,64,128]{2,1,0:T(8,128)(2,1)S(1)}, bf16[32,64,128]{2,1,0:T(8,128)(2,1)}, u32[]{:S(2)}) %copy-start.1) | copy-done | bytes 524312
  5.6 0.0 copy-start.2
  5.6 0.9 %copy-done.2 = f32[8,64,64]{2,1,0:T(8,128)S(1)} copy-done((f32[8,64,64]{2,1,0:T(8,128)S(1)}, f32[8,64,64]{2,1,0:T(8,128)}, u32[]{:S(2)}) %copy-start.2) | copy-done | bytes 131096
  6.6 56.2 %shard_map.104 = (bf16[32,128,128]{2,1,0:T(8,128)(2,1)S(1)}, f32[8,64]{1,0:T(8,128)S(1)}) custom-call(bf16[32,128,128]{2,1,0:T(8,128)(2,1)S(1)} %copy-done, s32[1,128]{1,0:T(1,128)S(1)} %bitcast.2, f32[8,64,64]{2,1,0:T(8,128)S(1)} %copy-done.2, bf16[32,64,128]{2,1,0:T(8,128)(2,1)S(1)} %copy-done.1, bf16[32,128]{1,0:T(8,128)(2,1)S(1)} %copy-done.3, ...), custom_call_target="tpu_custom_call" | custom-call | tf_op jit(solution)/shard_map/pallas_call | solution.py:276
  62.8 1.0 %copy.16 = bf16[32,128,128]{2,1,0:T(8,128)(2,1)} copy(bf16[32,128,128]{2,1,0:T(8,128)(2,1)S(1)} %get-tuple-element.4) | data formatting | bytes 2097152
  63.8 0.6 copy.17
Async XLA Ops:
  0.6 0.7 %copy-start.8 = (s32[32]{0:T(128)S(1)}, s32[32]{0:T(128)}, u32[]{:S(2)}) copy-start(s32[32]{0:T(128)} %param.14) | copy-start | bytes 388
  1.3 0.7 %copy-start.6 = (s32[128,8]{0,1:T(8,128)S(1)}, s32[128,8]{0,1:T(8,128)}, u32[]{:S(2)}) copy-start(s32[128,8]{0,1:T(8,128)} %param.15) | copy-start | bytes 12292
  2.0 0.7 %copy-start.7 = (s32[128,8]{0,1:T(8,128)S(1)}, s32[128,8]{0,1:T(8,128)}, u32[]{:S(2)}) copy-start(s32[128,8]{0,1:T(8,128)} %param.16) | copy-start | bytes 12292
  2.7 0.7 %copy-start.3 = (bf16[32,128]{1,0:T(8,128)(2,1)S(1)}, bf16[32,128]{1,0:T(8,128)(2,1)}, u32[]{:S(2)}) copy-start(bf16[32,128]{1,0:T(8,128)(2,1)} %dep_ref.1) | copy-start | bytes 24580
  2.7 0.7 %copy-start.4 = (f32[8,8]{1,0:T(8,128)S(1)}, f32[8,8]{1,0:T(8,128)}, u32[]{:S(2)}) copy-start(f32[8,8]{1,0:T(8,128)} %loc_ref.1) | copy-start | bytes 772
  2.7 0.7 %copy-start.5 = (s32[128]{0:T(128)S(1)}, s32[128]{0:T(128)}, u32[]{:S(2)}) copy-start(s32[128]{0:T(128)} %param.10) | copy-start | bytes 1540
  3.4 1.2 %copy-start = (bf16[32,128,128]{2,1,0:T(8,128)(2,1)S(1)}, bf16[32,128,128]{2,1,0:T(8,128)(2,1)}, u32[]{:S(2)}) copy-start(bf16[32,128,128]{2,1,0:T(8,128)(2,1)} %ens_ref.1) | copy-start | bytes 3145732
  4.6 1.0 %copy-start.1 = (bf16[32,64,128]{2,1,0:T(8,128)(2,1)S(1)}, bf16[32,64,128]{2,1,0:T(8,128)(2,1)}, u32[]{:S(2)}) copy-start(bf16[32,64,128]{2,1,0:T(8,128)(2,1)} %obs_ref.1) | copy-start | bytes 1572868
  5.6 0.9 %copy-start.2 = (f32[8,64,64]{2,1,0:T(8,128)S(1)}, f32[8,64,64]{2,1,0:T(8,128)}, u32[]{:S(2)}) copy-start(f32[8,64,64]{2,1,0:T(8,128)} %weights_ref.1) | copy-start | bytes 393220

commit v2 on v1

--- a/solution.py
+++ b/solution.py
@@ -33,11 +33,22 @@
 
 
 def peer_order(n):
-    return sorted(range(1, n), key=lambda k: -min(k, n - k))
+    return list(range(1, n))
 
 
 def fused_kernel(
     dims,
+    ens_hbm,
+    owner_hbm,
+    weights_hbm,
+    obs_hbm,
+    dep_hbm,
+    count_hbm,
+    home_hbm,
+    index_hbm,
+    loc_hbm,
+    out_hbm,
+    mw_hbm,
     ens_ref,
     owner_ref,
     weights_ref,
@@ -58,6 +69,9 @@
     scatter_mat,
     mix_mat,
     gain_ref,
+    load_sem,
+    ens_sem,
+    out_sem,
     obs_send,
     obs_recv,
     fwd_send,
@@ -70,7 +84,7 @@
     rows_here, blocks, points = ens_ref.shape
     block_dev, members, _ = weights_ref.shape
     obs_dev = obs_ref.shape[0]
-    pair_count = home_ref.shape[1]
+    pair_count = home_ref.shape[0]
     held = rows_here // LEV
     slab = held * block_dev
     full = n * slab
@@ -80,21 +94,110 @@
     peers = peer_order(n)
 
     barrier = pltpu.get_barrier_semaphore()
-
-    def greet(k, carry):
+    for k in peers:
         pl.semaphore_signal(
             barrier,
             inc=1,
             device_id={"grid": lax.rem(me + k, n)},
             device_id_type=pl.DeviceIdType.MESH,
         )
-        return carry
-
-    lax.fori_loop(1, n, greet, 0)
-
+
+    def level_rows(g, m):
+        return pl.ds(m * LEV + g * lev_group, lev_group)
+
+    def ens_load(g, m):
+        rows = level_rows(g, m)
+        return pltpu.make_async_copy(ens_hbm.at[rows], ens_ref.at[rows], ens_sem.at[g, m])
+
+    def out_store(g, m):
+        rows = level_rows(g, m)
+        return pltpu.make_async_copy(out_ref.at[rows], out_hbm.at[rows], out_sem.at[g, m])
+
+    small = (
+        (owner_hbm, owner_ref),
+        (obs_hbm, obs_ref),
+        (dep_hbm, dep_ref),
+        (count_hbm, count_ref),
+        (home_hbm, home_ref),
+        (index_hbm, index_ref),
+        (loc_hbm, loc_ref),
+        (weights_hbm, weights_ref),
+    )
+    loads = [
+        pltpu.make_async_copy(src, dst, load_sem.at[i]) for i, (src, dst) in enumerate(small)
+    ]
+    loads[0].start()
+    for g in range(groups):
+        for m in range(held):
+            ens_load(g, m).start()
+    for load in loads[1:]:
+        load.start()
+
+    r = iota((full, 1), 0)
+    row_key = (r // block_dev % held) * blocks + (r // slab) * block_dev + r % block_dev
+    loads[0].wait()
+    owner = jnp.concatenate([owner_ref[...]] * held, axis=1)
+    col_key = owner + iota((1, full), 1) // blocks * blocks
+    gather_mat[...] = one_hot(row_key == col_key)
+
+    def arrange(g):
+        for m in range(held):
+            ens_load(g, m).wait()
+        cols = []
+        for l in range(g * lev_group, (g + 1) * lev_group):
+            cols.append(
+                jnp.concatenate([ens_ref[m * LEV + l] for m in range(held)], axis=0)
+            )
+        state = jnp.concatenate(cols, axis=1)
+        sorted_state = dot(gather_mat[...], state).astype(BF16)
+        send_box[g] = sorted_state.reshape(n, slab, width)
+        recv_box[g, pl.ds(me, 1)] = send_box[g, pl.ds(me, 1)]
+
+    def obs_copy(k):
+        to = lax.rem(me + k, n)
+        return pltpu.make_async_remote_copy(
+            src_ref=obs_box.at[me],
+            dst_ref=obs_box.at[me],
+            send_sem=obs_send.at[k],
+            recv_sem=obs_recv.at[me],
+            device_id={"grid": to},
+            device_id_type=pl.DeviceIdType.MESH,
+        )
+
+    def box_copy(src, dst, send_sem, recv_sem, g, k):
+        to = lax.rem(me + k, n)
+        return pltpu.make_async_remote_copy(
+            src_ref=src.at[g, to],
+            dst_ref=dst.at[g, me],
+            send_sem=send_sem.at[g, k],
+            recv_sem=recv_sem.at[g, me],
+            device_id={"grid": to},
+            device_id_type=pl.DeviceIdType.MESH,
+        )
+
+    def box_arrival(dst, send_sem, recv_sem, g, k):
+        src = lax.rem(me + k, n)
+        return pltpu.make_async_remote_copy(
+            src_ref=dst.at[g, src],
+            dst_ref=dst.at[g, src],
+            send_sem=send_sem.at[g, k],
+            recv_sem=recv_sem.at[g, src],
+            device_id={"grid": src},
+            device_id_type=pl.DeviceIdType.MESH,
+        )
+
+    arrange(0)
+    pl.semaphore_wait(barrier, n - 1)
+    for k in peers:
+        box_copy(send_box, recv_box, fwd_send, fwd_recv, 0, k).start()
+
+    for load in loads[1:]:
+        load.wait()
     lane = iota((obs_dev, points), 1)
     dep = dep_ref[...].astype(F32)
-    masked = jnp.where(lane < count_ref[...], dep, 0.0).astype(BF16)
+    square = iota((obs_dev, obs_dev), 0) == iota((obs_dev, obs_dev), 1)
+    count = jnp.sum(jnp.where(square, count_ref[...], 0), axis=1, keepdims=True)
+    masked = jnp.where(lane < count, dep, 0.0).astype(BF16)
     cross = dot_nt(masked, obs_ref[...].reshape(obs_dev * members, points))
     row = iota((obs_dev, LANES), 0)
     lane_block = iota((obs_dev, LANES), 1) // members
@@ -106,62 +209,8 @@
     fold = one_hot(iota((packed, obs_dev), 0) == iota((packed, obs_dev), 1) // 2)
     obs_box[pl.ds(me, 1)] = dot(fold, sums.astype(BF16)).astype(BF16)[None]
 
-    r = iota((full, 1), 0)
-    row_key = (r // block_dev % held) * blocks + (r // slab) * block_dev + r % block_dev
-    owner = jnp.concatenate([owner_ref[...]] * held, axis=1)
-    col_key = owner + iota((1, full), 1) // blocks * blocks
-    gather_mat[...] = one_hot(row_key == col_key)
-
-    def arrange(g):
-        cols = []
-        for l in range(g * lev_group, (g + 1) * lev_group):
-            cols.append(
-                jnp.concatenate([ens_ref[m * LEV + l] for m in range(held)], axis=0)
-            )
-        state = jnp.concatenate(cols, axis=1)
-        sorted_state = dot(gather_mat[...], state).astype(BF16)
-        send_box[g] = sorted_state.reshape(n, slab, width)
-        recv_box[g, pl.ds(me, 1)] = send_box[g, pl.ds(me, 1)]
-
-    def obs_copy(k):
-        to = lax.rem(me + k, n)
-        return pltpu.make_async_remote_copy(
-            src_ref=obs_box.at[me],
-            dst_ref=obs_box.at[me],
-            send_sem=obs_send.at[k],
-            recv_sem=obs_recv.at[me],
-            device_id={"grid": to},
-            device_id_type=pl.DeviceIdType.MESH,
-        )
-
-    def box_copy(src, dst, send_sem, recv_sem, g, k):
-        to = lax.rem(me + k, n)
-        return pltpu.make_async_remote_copy(
-            src_ref=src.at[g, to],
-            dst_ref=dst.at[g, me],
-            send_sem=send_sem.at[g, k],
-            recv_sem=recv_sem.at[g, me],
-            device_id={"grid": to},
-            device_id_type=pl.DeviceIdType.MESH,
-        )
-
-    def box_arrival(dst, send_sem, recv_sem, g, k):
-        src = lax.rem(me + k, n)
-        return pltpu.make_async_remote_copy(
-            src_ref=dst.at[g, src],
-            dst_ref=dst.at[g, src],
-            send_sem=send_sem.at[g, k],
-            recv_sem=recv_sem.at[g, src],
-            device_id={"grid": src},
-            device_id_type=pl.DeviceIdType.MESH,
-        )
-
-    arrange(0)
-    pl.semaphore_wait(barrier, n - 1)
     for k in peers:
         obs_copy(k).start()
-    for k in peers:
-        box_copy(send_box, recv_box, fwd_send, fwd_recv, 0, k).start()
     for g in range(1, groups):
         arrange(g)
         for k in peers:
@@ -181,9 +230,11 @@
             device_id_type=pl.DeviceIdType.MESH,
         ).wait_recv()
     all_sums = obs_box[...].reshape(n * packed, LANES).astype(F32)
-    mine = pl.ds(pl.multiple_of(me * block_dev, block_dev), block_dev)
-    home = home_ref[mine, :]
-    index = index_ref[mine, :]
+    mine = one_hot(
+        iota((block_dev, blocks), 1) == iota((block_dev, blocks), 0) + me * block_dev
+    )
+    home = dot_nt(mine, home_ref[...].astype(F32).astype(BF16)).astype(jnp.int32)
+    index = dot_nt(mine, index_ref[...].astype(F32).astype(BF16)).astype(jnp.int32)
     spot = home * packed + index // 2
     odd = index % 2
     loc = loc_ref[...]
@@ -208,6 +259,8 @@
     projected = jnp.dot(spread, flat, precision=HIGHEST, preferred_element_type=F32)
     mean_w = jnp.sum(weights * projected[:, None, :], axis=2, keepdims=True) / (members - 1)
     mw_ref[...] = jnp.sum(weights * projected[:, None, :], axis=2) / (members - 1)
+    mw_store = pltpu.make_async_copy(mw_ref, mw_hbm, load_sem.at[len(loads)])
+    mw_store.start()
     transform = (weights + mean_w).astype(BF16).reshape(block_dev * members, members)
 
     rr = iota((full, full), 0)
@@ -243,7 +296,13 @@
                 out_ref[m * LEV + g * lev_group + l] = final[
                     m * blocks : (m + 1) * blocks, l * points : (l + 1) * points
                 ]
-
+        for m in range(held):
+            out_store(g, m).start()
+
+    mw_store.wait()
+    for g in range(groups):
+        for m in range(held):
+            out_store(g, m).wait()
     for k in peers:
         obs_copy(k).wait_send()
         for g in range(groups):
@@ -261,7 +320,7 @@
     pair_home,
     pair_index,
     localization,
-    groups=4,
+    groups=2,
 ):
     n = lax.axis_size("grid")
     rows_here, blocks, points = ensemble.shape
@@ -272,16 +331,30 @@
     width = LEV // groups * points
     obs_dev = obs_members.shape[0]
     box = pltpu.VMEM((groups, n, slab, width), BF16)
-    vmem = pl.BlockSpec(memory_space=pltpu.VMEM)
+    hbm = pl.BlockSpec(memory_space=pltpu.HBM)
+    operands = (
+        ensemble,
+        owner_slot.reshape(1, blocks),
+        weights,
+        obs_members,
+        departures,
+        obs_count.reshape(1, obs_dev),
+        pair_home.T,
+        pair_index.T,
+        localization,
+    )
     return pl.pallas_call(
         functools.partial(fused_kernel, (n, groups)),
         out_shape=(
             jax.ShapeDtypeStruct(ensemble.shape, BF16),
             jax.ShapeDtypeStruct((block_dev, members), F32),
         ),
-        in_specs=[vmem] * 9,
-        out_specs=(vmem, vmem),
+        in_specs=[hbm] * 9,
+        out_specs=(hbm, hbm),
         scratch_shapes=[
+            *[pltpu.VMEM(arg.shape, arg.dtype) for arg in operands],
+            pltpu.VMEM(ensemble.shape, BF16),
+            pltpu.VMEM((block_dev, members), F32),
             pltpu.VMEM((n, obs_dev // 2, LANES), BF16),
             box,
             box,
@@ -291,6 +364,9 @@
             pltpu.VMEM((full, full), BF16),
             pltpu.VMEM((full, full), BF16),
             pltpu.VMEM((full, width), F32),
+            pltpu.SemaphoreType.DMA((len(operands),)),
+            pltpu.SemaphoreType.DMA((groups, held)),
+            pltpu.SemaphoreType.DMA((groups, held)),
             pltpu.SemaphoreType.DMA((n,)),
             pltpu.SemaphoreType.DMA((n,)),
             pltpu.SemaphoreType.DMA((groups, n)),
@@ -299,19 +375,9 @@
             pltpu.SemaphoreType.DMA((groups, n)),
         ],
         compiler_params=pltpu.CompilerParams(
-            collective_id=0, has_side_effects=True, vmem_limit_bytes=40 * 2**20
+            collective_id=0, has_side_effects=True, vmem_limit_bytes=48 * 2**20
         ),
-    )(
-        ensemble,
-        owner_slot.reshape(1, blocks),
-        weights,
-        obs_members,
-        departures,
-        obs_count.reshape(obs_dev, 1),
-        pair_home,
-        pair_index,
-        localization,
-    )
+    )(*operands)
 
 
 def staged(

time: 64.7 us -> 63.1 us (0.975)
  the two profiles are of different devices: /device:TPU:0 before, /device:TPU:15 now
where the time goes in v2:
time: 63.1 us; the launch traced here: 62.8 us
  Pallas kernels  54.6 us (87%)
  local copies, waits for them, and re-layouts  7.52 us (12%)
  between operations  0.67 us (1%)
    pallas_call x1, Pallas kernels, fused(): pl.pallas_call(functools.partial(fused_kernel, (n, groups)), out_shape=(j...  54.6 us
    unnamed x20, local copies, waits for them, and re-layouts  7.52 us

profile of v2, /device:TPU:15, one launch (start us, length us, event | category | flops | bytes accessed | tf_op | source)
XLA Modules:
  0.0 62.8 jit_solution(14238505149720437348)
XLA Ops:
  0.6 0.0 copy-start.4
  0.6 0.0 copy-start.7
  0.7 0.0 copy-start.8
  0.7 0.7 %copy-done.4 = s32[128,8]{0,1:T(8,128)S(1)} copy-done((s32[128,8]{0,1:T(8,128)S(1)}, s32[128,8]{0,1:T(8,128)}, u32[]{:S(2)}) %copy-start.4) | copy-done | bytes 4120
  1.3 0.0 copy-done.7
  1.3 0.0 copy-done.8
  1.3 0.0 copy-start
  1.3 1.2 %copy-done = bf16[32,128,128]{2,1,0:T(8,128)(2,1)S(1)} copy-done((bf16[32,128,128]{2,1,0:T(8,128)(2,1)S(1)}, bf16[32,128,128]{2,1,0:T(8,128)(2,1)}, u32[]{:S(2)}) %copy-start) | copy-done | bytes 1048600
  2.6 0.0 copy-start.1
  2.6 1.0 %copy-done.1 = bf16[32,64,128]{2,1,0:T(8,128)(2,1)S(1)} copy-done((bf16[32,64,128]{2,1,0:T(8,128)(2,1)S(1)}, bf16[32,64,128]{2,1,0:T(8,128)(2,1)}, u32[]{:S(2)}) %copy-start.1) | copy-done | bytes 524312
  3.6 0.0 copy-start.2
  3.6 0.9 %copy-done.2 = f32[8,64,64]{2,1,0:T(8,128)S(1)} copy-done((f32[8,64,64]{2,1,0:T(8,128)S(1)}, f32[8,64,64]{2,1,0:T(8,128)}, u32[]{:S(2)}) %copy-start.2) | copy-done | bytes 131096
  4.5 0.0 copy-start.3
  4.5 0.7 %copy-done.3 = bf16[32,128]{1,0:T(8,128)(2,1)S(1)} copy-done((bf16[32,128]{1,0:T(8,128)(2,1)S(1)}, bf16[32,128]{1,0:T(8,128)(2,1)}, u32[]{:S(2)}) %copy-start.3) | copy-done | bytes 8216
  5.2 0.0 copy-start.5
  5.2 0.7 %copy-done.5 = s32[128,8]{0,1:T(8,128)S(1)} copy-done((s32[128,8]{0,1:T(8,128)S(1)}, s32[128,8]{0,1:T(8,128)}, u32[]{:S(2)}) %copy-start.5) | copy-done | bytes 4120
  5.9 0.0 copy-start.6
  5.9 0.7 %copy-done.6 = f32[8,8]{1,0:T(8,128)S(1)} copy-done((f32[8,8]{1,0:T(8,128)S(1)}, f32[8,8]{1,0:T(8,128)}, u32[]{:S(2)}) %copy-start.6) | copy-done | bytes 280
  6.6 54.6 %shard_map.104 = (bf16[32,128,128]{2,1,0:T(8,128)(2,1)S(1)}, f32[8,64]{1,0:T(8,128)S(1)}) custom-call(bf16[32,128,128]{2,1,0:T(8,128)(2,1)S(1)} %copy-done, s32[1,128]{1,0:T(1,128)S(1)} %bitcast.6, f32[8,64,64]{2,1,0:T(8,128)S(1)} %copy-done.2, bf16[32,64,128]{2,1,0:T(8,128)(2,1)S(1)} %copy-done.1, bf16[32,128]{1,0:T(8,128)(2,1)S(1)} %copy-done.3, ...), custom_call_target="tpu_custom_call" | custom-call | tf_op jit(solution)/shard_map/pallas_call | solution.py:346
  61.2 1.0 %copy.13 = bf16[32,128,128]{2,1,0:T(8,128)(2,1)} copy(bf16[32,128,128]{2,1,0:T(8,128)(2,1)S(1)} %get-tuple-element.4) | data formatting | bytes 2097152
  62.2 0.6 copy.14
Async XLA Ops:
  0.6 0.7 %copy-start.4 = (s32[128,8]{0,1:T(8,128)S(1)}, s32[128,8]{0,1:T(8,128)}, u32[]{:S(2)}) copy-start(s32[128,8]{0,1:T(8,128)} %param.15) | copy-start | bytes 12292
  0.6 0.7 %copy-start.7 = (s32[128]{0:T(128)S(1)}, s32[128]{0:T(128)}, u32[]{:S(2)}) copy-start(s32[128]{0:T(128)} %param.10) | copy-start | bytes 1540
  0.7 0.7 %copy-start.8 = (s32[32]{0:T(128)S(1)}, s32[32]{0:T(128)}, u32[]{:S(2)}) copy-start(s32[32]{0:T(128)} %param.14) | copy-start | bytes 388
  1.3 1.2 %copy-start = (bf16[32,128,128]{2,1,0:T(8,128)(2,1)S(1)}, bf16[32,128,128]{2,1,0:T(8,128)(2,1)}, u32[]{:S(2)}) copy-start(bf16[32,128,128]{2,1,0:T(8,128)(2,1)} %ens_hbm.1) | copy-start | bytes 3145732
  2.6 1.0 %copy-start.1 = (bf16[32,64,128]{2,1,0:T(8,128)(2,1)S(1)}, bf16[32,64,128]{2,1,0:T(8,128)(2,1)}, u32[]{:S(2)}) copy-start(bf16[32,64,128]{2,1,0:T(8,128)(2,1)} %obs_hbm.1) | copy-start | bytes 1572868
  3.6 0.9 %copy-start.2 = (f32[8,64,64]{2,1,0:T(8,128)S(1)}, f32[8,64,64]{2,1,0:T(8,128)}, u32[]{:S(2)}) copy-start(f32[8,64,64]{2,1,0:T(8,128)} %weights_hbm.1) | copy-start | bytes 393220
  4.5 0.7 %copy-start.3 = (bf16[32,128]{1,0:T(8,128)(2,1)S(1)}, bf16[32,128]{1,0:T(8,128)(2,1)}, u32[]{:S(2)}) copy-start(bf16[32,128]{1,0:T(8,128)(2,1)} %dep_hbm.1) | copy-start | bytes 24580
  5.2 0.7 %copy-start.5 = (s32[128,8]{0,1:T(8,128)S(1)}, s32[128,8]{0,1:T(8,128)}, u32[]{:S(2)}) copy-start(s32[128,8]{0,1:T(8,128)} %param.16) | copy-start | bytes 12292
  5.9 0.7 %copy-start.6 = (f32[8,8]{1,0:T(8,128)S(1)}, f32[8,8]{1,0:T(8,128)}, u32[]{:S(2)}) copy-start(f32[8,8]{1,0:T(8,128)} %loc_hbm.1) | copy-start | bytes 772

commit v3 on v2

--- a/solution.py
+++ b/solution.py
@@ -375,7 +375,7 @@
             pltpu.SemaphoreType.DMA((groups, n)),
         ],
         compiler_params=pltpu.CompilerParams(
-            collective_id=0, has_side_effects=True, vmem_limit_bytes=48 * 2**20
+            collective_id=0, has_side_effects=True, vmem_limit_bytes=60 * 2**20
         ),
     )(*operands)
 

time: 63.1 us -> 58.6 us (0.929)
  local copies, waits for them, and re-layouts: 7.52 us -> 2.9 us
    unnamed x20 -> x4, local copies, waits for them, and re-layouts: 7.52 us -> 2.9 us
where the time goes in v3:
time: 58.6 us; the launch traced here: 58.5 us
  Pallas kernels  54.9 us (94%)
  local copies, waits for them, and re-layouts  2.9 us (5%)
  between operations  0.65 us (1%)
    pallas_call x1, Pallas kernels, fused(): pl.pallas_call(functools.partial(fused_kernel, (n, groups)), out_shape=(j...  54.9 us
    unnamed x4, local copies, waits for them, and re-layouts  2.9 us

profile of v3, /device:TPU:15, one launch (start us, length us, event | category | flops | bytes accessed | tf_op | source)
XLA Modules:
  0.0 58.5 jit_solution(6377163519869769415)
XLA Ops:
  0.6 54.9 %shard_map.104 = (bf16[32,128,128]{2,1,0:T(8,128)(2,1)}, f32[8,64]{1,0:T(8,128)}) custom-call(bf16[32,128,128]{2,1,0:T(8,128)(2,1)} %ens_hbm.1, s32[1,128]{1,0:T(1,128)} %bitcast.6, f32[8,64,64]{2,1,0:T(8,128)} %weights_hbm.1, bf16[32,64,128]{2,1,0:T(8,128)(2,1)} %obs_hbm.1, bf16[32,128]{1,0:T(8,128)(2,1)} %dep_hbm.1, s32[1,32]{1,0:T(1,128)} %bitcast.7, ...), custom_call_target="tpu_custom_call" | custom-call | tf_op jit(solution)/shard_map/pallas_call | solution.py:346
  55.5 0.0 copy-start
  55.6 2.3 %copy.13 = bf16[32,128,128]{2,1,0:T(8,128)(2,1)} copy(bf16[32,128,128]{2,1,0:T(8,128)(2,1)} %get-tuple-element.4) | data formatting | bytes 2097152
  57.9 0.0 copy-done
  57.9 0.6 %copy.14 = f32[8,64]{1,0:T(8,128)} copy(f32[8,64]{1,0:T(8,128)S(1)} %copy-done) | data formatting | bytes 4096
Async XLA Ops:
  55.5 2.3 %copy-start = (f32[8,64]{1,0:T(8,128)S(1)}, f32[8,64]{1,0:T(8,128)}, u32[]{:S(2)}) copy-start(f32[8,64]{1,0:T(8,128)} %get-tuple-element.5) | copy-start | bytes 6148

commit v4 on v3

--- a/solution.py
+++ b/solution.py
@@ -47,7 +47,8 @@
     home_hbm,
     index_hbm,
     loc_hbm,
-    out_hbm,
+    back_box,
+    scatter_hbm,
     mw_hbm,
     ens_ref,
     owner_ref,
@@ -58,20 +59,18 @@
     home_ref,
     index_ref,
     loc_ref,
-    out_ref,
     mw_ref,
     obs_box,
     send_box,
     recv_box,
     ret_box,
-    back_box,
     gather_mat,
     scatter_mat,
     mix_mat,
     gain_ref,
     load_sem,
     ens_sem,
-    out_sem,
+    own_sem,
     obs_send,
     obs_recv,
     fwd_send,
@@ -109,9 +108,8 @@
         rows = level_rows(g, m)
         return pltpu.make_async_copy(ens_hbm.at[rows], ens_ref.at[rows], ens_sem.at[g, m])
 
-    def out_store(g, m):
-        rows = level_rows(g, m)
-        return pltpu.make_async_copy(out_ref.at[rows], out_hbm.at[rows], out_sem.at[g, m])
+    def own_return(g):
+        return pltpu.make_async_copy(ret_box.at[g, me], back_box.at[g, me], own_sem.at[g])
 
     small = (
         (owner_hbm, owner_ref),
@@ -218,6 +216,8 @@
 
     same = one_hot(iota((full, full), 0) == iota((full, full), 1))
     scatter_mat[...] = dot_nt(same, gather_mat[...]).astype(BF16)
+    scatter_store = pltpu.make_async_copy(scatter_mat, scatter_hbm, load_sem.at[len(loads)])
+    scatter_store.start()
 
     for k in peers:
         src = lax.rem(me + k, n)
@@ -259,7 +259,7 @@
     projected = jnp.dot(spread, flat, precision=HIGHEST, preferred_element_type=F32)
     mean_w = jnp.sum(weights * projected[:, None, :], axis=2, keepdims=True) / (members - 1)
     mw_ref[...] = jnp.sum(weights * projected[:, None, :], axis=2) / (members - 1)
-    mw_store = pltpu.make_async_copy(mw_ref, mw_hbm, load_sem.at[len(loads)])
+    mw_store = pltpu.make_async_copy(mw_ref, mw_hbm, load_sem.at[len(loads) + 1])
     mw_store.start()
     transform = (weights + mean_w).astype(BF16).reshape(block_dev * members, members)
 
@@ -283,31 +283,73 @@
         gain = gain_ref[...].reshape(members, block_dev, width)
         analysis = (product + gain * member_sum[None]).astype(BF16)
         ret_box[g] = analysis.reshape(n, slab, width)
-        back_box[g, pl.ds(me, 1)] = ret_box[g, pl.ds(me, 1)]
+        own_return(g).start()
         for k in peers:
             box_copy(ret_box, back_box, bwd_send, bwd_recv, g, k).start()
 
-    for g in range(groups):
-        for k in peers:
-            box_arrival(back_box, bwd_send, bwd_recv, g, n - k).wait_recv()
-        final = dot(scatter_mat[...], back_box[g].reshape(full, width)).astype(BF16)
-        for l in range(lev_group):
-            for m in range(held):
-                out_ref[m * LEV + g * lev_group + l] = final[
-                    m * blocks : (m + 1) * blocks, l * points : (l + 1) * points
-                ]
-        for m in range(held):
-            out_store(g, m).start()
-
-    mw_store.wait()
-    for g in range(groups):
-        for m in range(held):
-            out_store(g, m).wait()
     for k in peers:
         obs_copy(k).wait_send()
         for g in range(groups):
             box_copy(send_box, recv_box, fwd_send, fwd_recv, g, k).wait_send()
             box_copy(ret_box, back_box, bwd_send, bwd_recv, g, k).wait_send()
+    scatter_store.wait()
+    mw_store.wait()
+    for g in range(groups):
+        own_return(g).wait()
+        for k in peers:
+            box_arrival(back_box, bwd_send, bwd_recv, g, n - k).wait_recv()
+
+
+def restore_kernel(
+    back_hbm,
+    scatter_hbm,
+    mw_hbm,
+    out_hbm,
+    mw_out,
+    back_ref,
+    scatter_ref,
+    mw_ref,
+    out_ref,
+    fixed_sem,
+    in_sem,
+    out_sem,
+):
+    groups, n, slab, width = back_ref.shape
+    held, _, blocks, points = out_ref.shape
+    lev_group = width // points
+    scatter_load = pltpu.make_async_copy(scatter_hbm, scatter_ref, fixed_sem.at[0])
+    mw_load = pltpu.make_async_copy(mw_hbm, mw_ref, fixed_sem.at[1])
+    mw_store = pltpu.make_async_copy(mw_ref, mw_out, fixed_sem.at[2])
+
+    def load(g):
+        return pltpu.make_async_copy(back_hbm.at[g], back_ref.at[g], in_sem.at[g])
+
+    def store(l):
+        return pltpu.make_async_copy(out_ref.at[:, l], out_hbm.at[:, l], out_sem.at[l])
+
+    scatter_load.start()
+    for g in range(groups):
+        load(g).start()
+    mw_load.start()
+    mw_load.wait()
+    mw_store.start()
+    scatter_load.wait()
+    step = 2 * points
+    for g in range(groups):
+        load(g).wait()
+        for c in range(width // step):
+            state = back_ref[g, :, :, c * step : (c + 1) * step].reshape(n * slab, step)
+            final = dot(scatter_ref[...], state).astype(BF16)
+            for t in range(2):
+                l = g * lev_group + c * 2 + t
+                for m in range(held):
+                    out_ref[m, l] = final[
+                        m * blocks : (m + 1) * blocks, t * points : (t + 1) * points
+                    ]
+                store(l).start()
+    mw_store.wait()
+    for l in range(LEV):
+        store(l).wait()
 
 
 def fused(
@@ -343,20 +385,19 @@
         pair_index.T,
         localization,
     )
-    return pl.pallas_call(
+    back, scatter, mean_weights = pl.pallas_call(
         functools.partial(fused_kernel, (n, groups)),
         out_shape=(
-            jax.ShapeDtypeStruct(ensemble.shape, BF16),
+            jax.ShapeDtypeStruct((groups, n, slab, width), BF16),
+            jax.ShapeDtypeStruct((full, full), BF16),
             jax.ShapeDtypeStruct((block_dev, members), F32),
         ),
         in_specs=[hbm] * 9,
-        out_specs=(hbm, hbm),
+        out_specs=(hbm, hbm, hbm),
         scratch_shapes=[
             *[pltpu.VMEM(arg.shape, arg.dtype) for arg in operands],
-            pltpu.VMEM(ensemble.shape, BF16),
             pltpu.VMEM((block_dev, members), F32),
             pltpu.VMEM((n, obs_dev // 2, LANES), BF16),
-            box,
             box,
             box,
             box,
@@ -364,9 +405,9 @@
             pltpu.VMEM((full, full), BF16),
             pltpu.VMEM((full, full), BF16),
             pltpu.VMEM((full, width), F32),
-            pltpu.SemaphoreType.DMA((len(operands),)),
+            pltpu.SemaphoreType.DMA((len(operands) + 1,)),
             pltpu.SemaphoreType.DMA((groups, held)),
-            pltpu.SemaphoreType.DMA((groups, held)),
+            pltpu.SemaphoreType.DMA((groups,)),
             pltpu.SemaphoreType.DMA((n,)),
             pltpu.SemaphoreType.DMA((n,)),
             pltpu.SemaphoreType.DMA((groups, n)),
@@ -378,6 +419,26 @@
             collective_id=0, has_side_effects=True, vmem_limit_bytes=60 * 2**20
         ),
     )(*operands)
+    analysis, mean_weights = pl.pallas_call(
+        restore_kernel,
+        out_shape=(
+            jax.ShapeDtypeStruct((held, LEV, blocks, points), BF16),
+            jax.ShapeDtypeStruct((block_dev, members), F32),
+        ),
+        in_specs=[hbm] * 3,
+        out_specs=(hbm, hbm),
+        scratch_shapes=[
+            pltpu.VMEM((groups, n, slab, width), BF16),
+            pltpu.VMEM((full, full), BF16),
+            pltpu.VMEM((block_dev, members), F32),
+            pltpu.VMEM((held, LEV, blocks, points), BF16),
+            pltpu.SemaphoreType.DMA((3,)),
+            pltpu.SemaphoreType.DMA((groups,)),
+            pltpu.SemaphoreType.DMA((LEV,)),
+        ],
+        compiler_params=pltpu.CompilerParams(vmem_limit_bytes=60 * 2**20),
+    )(back, scatter, mean_weights)
+    return analysis.reshape(ensemble.shape), mean_weights
 
 
 def staged(

time: 58.6 us -> 57.5 us (0.981)
  local copies, waits for them, and re-layouts: 2.9 us -> 0 us
  Pallas kernels: 54.9 us -> 56.7 us
    pallas_call x0 -> x1, Pallas kernels: none -> 3.05 us  [fused(): pl.pallas_call(restore_kernel, out_shape=(jax.ShapeDtypeStruct((held, LEV...]
    unnamed x4 -> x0, local copies, waits for them, and re-layouts: 2.9 us -> none
    pallas_call x1, Pallas kernels: 54.9 us -> 53.6 us  [fused(): pl.pallas_call(functools.partial(fused_kernel, (n, groups)), out_shape=(j...]
where the time goes in v4:
time: 57.5 us; the launch traced here: 57.3 us
  Pallas kernels  56.7 us (99%)
  between operations  0.64 us (1%)
    pallas_call x1, Pallas kernels, fused(): pl.pallas_call(functools.partial(fused_kernel, (n, groups)), out_shape=(j...  53.6 us
    pallas_call x1, Pallas kernels, fused(): pl.pallas_call(restore_kernel, out_shape=(jax.ShapeDtypeStruct((held, LEV...  3.05 us

profile of v4, /device:TPU:15, one launch (start us, length us, event | category | flops | bytes accessed | tf_op | source)
XLA Modules:
  0.0 57.3 jit_solution(14731443923341973461)
XLA Ops:
  0.6 53.6 %shard_map.104 = (bf16[2,16,32,512]{3,2,1,0:T(8,128)(2,1)}, bf16[512,512]{1,0:T(8,128)(2,1)}, f32[8,64]{1,0:T(8,128)}) custom-call(bf16[32,128,128]{2,1,0:T(8,128)(2,1)} %ens_hbm.1, s32[1,128]{1,0:T(1,128)} %bitcast.7, f32[8,64,64]{2,1,0:T(8,128)} %weights_hbm.1, bf16[32,64,128]{2,1,0:T(8,128)(2,1)} %obs_hbm.1, bf16[32,128]{1,0:T(8,128)(2,1)} %dep_hbm.1, ...), custom_call_target="tpu_custom_call" | custom-call | tf_op jit(solution)/shard_map/pallas_call | solution.py:388
  54.3 3.0 %shard_map.105 = (bf16[4,8,128,128]{3,2,1,0:T(8,128)(2,1)}, f32[8,64]{1,0:T(8,128)}) custom-call(bf16[2,16,32,512]{3,2,1,0:T(8,128)(2,1)} %get-tuple-element.7.back_hbm, bf16[512,512]{1,0:T(8,128)(2,1)} %get-tuple-element.8.scatter_hbm, f32[8,64]{1,0:T(8,128)} %get-tuple-element.9.mw_hbm), custom_call_target="tpu_custom_call" | custom-call | tf_op jit(solution)/shard_map/pallas_call | solution.py:422

commit v5 on v4

--- a/solution.py
+++ b/solution.py
@@ -33,7 +33,7 @@
 
 
 def peer_order(n):
-    return list(range(1, n))
+    return [(n // 4 - 1 + k) % (n - 1) + 1 for k in range(n - 1)]
 
 
 def fused_kernel(
@@ -327,14 +327,12 @@
     def store(l):
         return pltpu.make_async_copy(out_ref.at[:, l], out_hbm.at[:, l], out_sem.at[l])
 
+    step = 2 * points
     scatter_load.start()
     for g in range(groups):
         load(g).start()
     mw_load.start()
-    mw_load.wait()
-    mw_store.start()
     scatter_load.wait()
-    step = 2 * points
     for g in range(groups):
         load(g).wait()
         for c in range(width // step):
@@ -347,6 +345,8 @@
                         m * blocks : (m + 1) * blocks, t * points : (t + 1) * points
                     ]
                 store(l).start()
+    mw_load.wait()
+    mw_store.start()
     mw_store.wait()
     for l in range(LEV):
         store(l).wait()

time: 57.5 us -> 57.2 us (level)
  no operation moved by 1% of the time
where the time goes in v5:
time: 57.2 us; the launch traced here: 57.1 us
  Pallas kernels  56.4 us (99%)
  between operations  0.64 us (1%)
    pallas_call x1, Pallas kernels, fused(): pl.pallas_call(functools.partial(fused_kernel, (n, groups)), out_shape=(j...  53.4 us
    pallas_call x1, Pallas kernels, fused(): pl.pallas_call(restore_kernel, out_shape=(jax.ShapeDtypeStruct((held, LEV...  3.01 us

profile of v5, /device:TPU:15, one launch (start us, length us, event | category | flops | bytes accessed | tf_op | source)
XLA Modules:
  0.0 57.1 jit_solution(11165795923389597087)
XLA Ops:
  0.6 53.4 %shard_map.104 = (bf16[2,16,32,512]{3,2,1,0:T(8,128)(2,1)}, bf16[512,512]{1,0:T(8,128)(2,1)}, f32[8,64]{1,0:T(8,128)}) custom-call(bf16[32,128,128]{2,1,0:T(8,128)(2,1)} %ens_hbm.1, s32[1,128]{1,0:T(1,128)} %bitcast.7, f32[8,64,64]{2,1,0:T(8,128)} %weights_hbm.1, bf16[32,64,128]{2,1,0:T(8,128)(2,1)} %obs_hbm.1, bf16[32,128]{1,0:T(8,128)(2,1)} %dep_hbm.1, ...), custom_call_target="tpu_custom_call" | custom-call | tf_op jit(solution)/shard_map/pallas_call | solution.py:388
  54.0 3.0 %shard_map.105 = (bf16[4,8,128,128]{3,2,1,0:T(8,128)(2,1)}, f32[8,64]{1,0:T(8,128)}) custom-call(bf16[2,16,32,512]{3,2,1,0:T(8,128)(2,1)} %get-tuple-element.7.back_hbm, bf16[512,512]{1,0:T(8,128)(2,1)} %get-tuple-element.8.scatter_hbm, f32[8,64]{1,0:T(8,128)} %get-tuple-element.9.mw_hbm), custom_call_target="tpu_custom_call" | custom-call | tf_op jit(solution)/shard_map/pallas_call | solution.py:422
